TPU v7x, 1024 devices: a whole 4x8x16 slice. The times are simulated.
1024 devices in a mesh: fsdp: 16 (over y_lo, x), tensor: 64 (over z, y_hi, core).
Axes of the slice: x: 4, y: 8 (y_hi: 2, y_lo: 4; y = y_hi * 4 + y_lo), z: 16, core: 2. Of those that a mesh axis runs over, the one named last changes fastest.
Arguments:
- tokens: bfloat16 [4096, 8192], P(('fsdp', 'tensor')), may hold values from -6 to 6
- weight_codes: bfloat16 [8192, 8192], P('fsdp', 'tensor'), may hold values from -6 to 6
- block_scales: bfloat16 [64, 64], P('fsdp', 'tensor'), may hold values from 0.0049743652 to 0.024902344
- grad_out: bfloat16 [4096, 8192], P('fsdp', 'tensor'), may hold values from -0.119628906 to 0.119628906
Outputs:
- projected: bfloat16 [4096, 8192], P('fsdp', 'tensor')
- weight_grad: bfloat16 [8192, 8192], P('fsdp', 'tensor')
All inputs are finite; a program needn't handle non-finite values.
Results may differ from a plain program's by a relative error of at most 0.0049.
Values may be sent and summed in bfloat16 or wider, within the bound.
A program may use at most 32 MiB of HBM per device.

v0:
```python
import jax
import jax.numpy as jnp
from jax import lax
from jax.sharding import PartitionSpec as P

BLOCK = 128


def dequantize(codes_part, scales_part):
    expanded = jnp.repeat(scales_part.astype(jnp.float32), BLOCK, axis=1)[:, None, :]
    weight = (codes_part.astype(jnp.float32) * expanded).astype(jnp.bfloat16)
    return weight.reshape(-1, weight.shape[2])


def per_device(tokens, weight_codes, block_scales, grad_out):
    col_count = weight_codes.shape[1]
    blocked = weight_codes.reshape(-1, BLOCK, col_count)
    gathered = lax.all_gather(tokens, "tensor", axis=0, tiled=True)
    weight = dequantize(
        lax.all_gather(blocked, "fsdp", axis=0, tiled=True),
        lax.all_gather(block_scales, "fsdp", axis=0, tiled=True),
    )
    columns = gathered
    projected = jnp.dot(columns, weight, preferred_element_type=jnp.float32)
    columns = gathered
    summed = lax.psum_scatter(
        lax.dot_general(
            columns, grad_out, (((0,), (0,)), ((), ())), preferred_element_type=jnp.float32
        ),
        "fsdp",
        scatter_dimension=0,
        tiled=True,
    )
    return (projected.astype(jnp.bfloat16), summed.astype(jnp.bfloat16))


def solution(mesh):
    in_specs = (
        P(("fsdp", "tensor"), None),
        P("fsdp", "tensor"),
        P("fsdp", "tensor"),
        P("fsdp", "tensor"),
    )
    out_specs = (P("fsdp", "tensor"), P("fsdp", "tensor"))
    return jax.shard_map(
        per_device, mesh=mesh, in_specs=in_specs, out_specs=out_specs, check_vma=False
    )
```

profile of v0, /device:TPU:64, one launch (start us, length us, event | category | flops | bytes accessed | tf_op | source)
XLA Modules:
  0.0 388.3 jit_solution(9955504811649902686)
XLA Ops:
  7.2 0.0 copy-start
  7.2 0.0 all-gather.6.cloned.1.call-start
  7.2 0.7 all-gather.6.cloned.1.call-update
  7.9 0.0 all-gather.4.cloned.1.call-start
  8.0 0.7 all-gather.4.cloned.1.call-update
  8.7 0.0 reduce-scatter.2.cloned.1.call-start
  8.7 182.3 %all-gather.6.cloned.1.call-done = bf16[64,4,8192]{2,1,0:T(4,128)(2,1)} async-done(((bf16[1,4,8192]{2,1,0:T(4,128)(2,1)}), bf16[64,4,8192]{2,1,0:T(4,128)(2,1)}) %all-gather.6.cloned.1.call-update) | async-done | bytes 4194320 | tf_op jit(solution)/shard_map/all_gather | solution.py:18
  191.0 6.9 %reshape.19 = bf16[256,8192]{1,0:T(8,128)(2,1)} reshape(bf16[64,4,8192]{2,1,0:T(4,128)(2,1)} %all-gather.6.cloned.1.call-done) | data formatting | bytes 8388608
  197.9 0.0 copy-done
  197.9 5.5 %fusion.1 = f32[8192,128]{1,0:T(8,128)} fusion(bf16[256,8192]{1,0:T(8,128)(2,1)} %reshape.19, bf16[256,128]{1,0:T(8,128)(2,1)S(1)} %copy-done), kind=kOutput, calls=%fused_computation.3 | convolution fusion | flops 536870912 | bytes 8454144 | tf_op jit(solution)/shard_map/dot_general | solution.py:27
  203.4 0.0 copy-start.2
  203.4 0.0 reduce-scatter.2.cloned.1.call-update
  203.4 1.3 dynamic-slice
  205.3 0.0 copy-done.2
  205.4 0.2 dynamic-update-slice
  205.6 39.3 %all-reduce = bf16[64]{0:T(256)(128)(2,1)S(1)} all-reduce(bf16[64]{0:T(256)(128)(2,1)S(1)} %dynamic-update-slice), channel_id=1, replica_groups=mesh['fsdp'=16,'tensor'=64] {'fsdp'}, use_global_device_ids=true, to_apply=%add | all-reduce | flops 64 | bytes 256
  244.9 31.0 %all-gather.4.cloned.1.call-done = bf16[64,128,128]{2,1,0:T(8,128)(2,1)} async-done(((bf16[4,128,128]{2,1,0:T(8,128)(2,1)}), bf16[64,128,128]{2,1,0:T(8,128)(2,1)}) %all-gather.4.cloned.1.call-update) | async-done | bytes 2097168 | tf_op jit(solution)/shard_map/all_gather | solution.py:20
  276.0 0.0 copy-start.1
  276.0 2.2 multiply_convert_fusion
  278.2 0.6 copy-done.1
  278.8 1.5 fusion
  280.3 0.7 copy.7
  281.1 99.1 %reduce-scatter.2.cloned.1.call-done = f32[512,128]{1,0:T(8,128)} async-done(((f32[8192,128]{1,0:T(8,128)}), f32[512,128]{1,0:T(8,128)}) %reduce-scatter.2.cloned.1.call-update) | async-done | bytes 262160 | tf_op jit(solution)/shard_map/reduce_scatter | solution.py:26
  380.2 1.6 convert_element_type.26
  (2 shorter events, 0.0 us)
Async XLA Ops:
  7.2 190.7 %copy-start = (bf16[256,128]{1,0:T(8,128)(2,1)S(1)}, bf16[256,128]{1,0:T(8,128)(2,1)}, u32[]{:S(2)}) copy-start(bf16[256,128]{1,0:T(8,128)(2,1)} %param.7) | copy-start | bytes 196612
  7.2 183.8 %all-gather.6.cloned.1.call-start = ((), (), s32[]{:S(2)}) async-start(), calls=%async_computation.3 | async-start | bytes 4259840 | tf_op jit(solution)/shard_map/all_gather | solution.py:18
  7.9 268.0 %all-gather.4.cloned.1.call-start = ((), (), s32[]{:S(2)}) async-start(), calls=%async_computation.1 | async-start | bytes 2228224 | tf_op jit(solution)/shard_map/all_gather | solution.py:20
  8.7 371.5 %reduce-scatter.2.cloned.1.call-start = ((), (), s32[]{:S(2)}) async-start(), calls=%async_computation.2 | async-start | bytes 4456448 | tf_op jit(solution)/shard_map/reduce_scatter | solution.py:26
  203.4 2.0 copy-start.2
  276.0 2.8 copy-start.1
Sparse Core Ops, SparseCore 0:
  12.5 178.5 all-gather.5
  193.7 82.2 all-gather.3
  279.4 100.7 reduce-scatter.1
where the time goes:
time: 389 us; the launch traced here: 388 us
  waiting for transfers between devices  314 us (81%)
  blocking collectives  39.3 us (10%)
  between operations  14.4 us (4%)
  local copies, waits for them, and re-layouts  9.75 us (3%)
  matrix products  7.01 us (2%)
    all_gather x1, waiting for transfers between devices, per_device(): gathered = lax.all_gather(tokens, 'tensor', axis=0, tiled=True)  182 us
    reduce_scatter x1, waiting for transfers between devices, per_device(): lax.psum_scatter(lax.dot_general(columns, grad_out, (((0,), (0,)), ((), (...  99.1 us
    unnamed x1, blocking collectives  39.3 us
    all_gather x1, waiting for transfers between devices, per_device(): lax.all_gather(blocked, 'fsdp', axis=0, tiled=True)  31 us
    unnamed x11, local copies, waits for them, and re-layouts  9.75 us
  transfers between devices with their start and end apart: 3, of which 3 were waited for; matrix products, arithmetic and copies ran while one was open for 5% of the time, Pallas kernels for 0%

commit v1 on v0

v1 whole, which is shorter than its diff:
```python
import jax
import jax.numpy as jnp
from jax import lax
from jax.experimental import pallas as pl
from jax.experimental.pallas import tpu as pltpu
from jax.sharding import PartitionSpec as P

MESH = pl.DeviceIdType.MESH
NX, NY, NZ, YL = 4, 8, 16, 4
SUB = 2
B16, F32 = jnp.bfloat16, jnp.float32

GROUPS = ((0, 1, -1, 2), (-2, 3, -3, 4), (-4, 5, -5, 6), (-6, 7, -7, -8))
FORWARD = {0: (1,), 1: (2,), 2: (3,), 3: (4,), 4: (5,), 5: (6,), 6: (7,), 7: (8,), 8: ()}
Z_STEPS = sorted({b - a for a, bs in FORWARD.items() for b in bs})
SWAPS = [(dy, dc) for dy in range(NY) for dc in range(2) if dy or dc]


def at(x, y, z, c):
    return ((y % YL) * NX + x, z * 4 + (y // YL) * 2 + c)


def kernel(
    tok, codes, scales, grad, out_p, out_w,
    s32, s16, a16, t32, t16, ws, wg, gg, ps, rp, dd, ds, rd, es, rw,
    a_s, a_r, w_s, w_r, v_s, v_r, g_s, g_r, z_s, z_r, c_s, c_r, p_s, p_r, d_s, d_r, e_s, e_r,
):
    f, t = lax.axis_index("fsdp"), lax.axis_index("tensor")
    x, y, z, c = f % NX, (t // 2) % 2 * YL + f // NX, t // 4, t % 2
    sent = []

    def send(src, dst, send_sem, recv_sem, device):
        copy = pltpu.make_async_remote_copy(
            src_ref=src, dst_ref=dst, send_sem=send_sem, recv_sem=recv_sem,
            device_id=device, device_id_type=MESH,
        )
        copy.start()
        sent.append(copy)
        return copy

    barrier = pltpu.get_barrier_semaphore()
    partners = [at(x, (y + dy) % NY, z, (c + dc) % 2) for dy, dc in SWAPS]
    partners += [at((x + dx) % NX, y, z, c) for dx in range(1, NX)]
    partners += [at(x, y, (z + dz) % NZ, c) for s in Z_STEPS for dz in (s, NZ - s)]
    for device in partners:
        pl.semaphore_signal(barrier, inc=1, device_id=device, device_id_type=MESH)

    rows = tok[...].astype(F32)
    for dest in range(2 * NY):
        yy, cc = dest // 2, dest % 2
        for j in range(NX):
            b = ((yy + 2) % YL) * 16 + j * 4 + (yy // YL) * 2 + cc
            s32[dest, j * 4 : j * 4 + 4, :] = rows[:, b * 128 : b * 128 + 128]
    s16[...] = s32[...].astype(B16)
    scale = scales[...].astype(F32)
    for b in range(4):
        block = codes[b * 128 : b * 128 + 128, :].astype(F32) * scale[b : b + 1, 0:1]
        ws[b // 2, (b % 2) * 128 : (b % 2) * 128 + 128, :] = block.astype(B16)

    pl.semaphore_wait(barrier, len(partners))

    me = y * 2 + c
    swaps = []
    for k, (dy, dc) in enumerate(SWAPS):
        yy, cc = (y + dy) % NY, (c + dc) % 2
        swaps.append(
            send(s16.at[yy * 2 + cc], a16.at[me], a_s.at[k], a_r.at[k], at(x, yy, z, cc))
        )
    a16[me] = s16[me]
    w_in = []
    for k, e in enumerate((2, 6)):
        yy = (y + e) % NY
        w_in.append(
            send(ws.at[yy // YL], wg.at[x, y // YL], w_s.at[k], w_r.at[k], at(x, yy, z, c))
        )

    for copy in swaps:
        copy.wait_recv()
    for src in range(2 * NY):
        yy, cc = src // 2, src % 2
        piece = a16[src].astype(F32)
        for j in range(NX):
            r = ((yy // YL) * 2 + cc) * 4
            t32[yy % YL, r : r + 4, j * 128 : j * 128 + 128] = piece[j * 4 : j * 4 + 4, :]
    t16[0, c] = t32[...].astype(B16)

    z_in, c_in = {}, {}

    def part(d, s):
        n = YL // SUB
        return t16.at[d % NZ, c, s * n : s * n + n]

    def forward(d, s):
        ways = (1, -1) if d == 0 else ((1,) if d < 0 else (-1,))
        for way in ways:
            for far in FORWARD[abs(d)]:
                if far == NZ // 2 and way < 0:
                    continue
                to = -way * far
                step = to - d
                z_in[to, s] = send(
                    part(d, s), part(to, s), z_s.at[to % NZ, s], z_r.at[to % NZ, s],
                    at(x, y, (z - step) % NZ, c),
                )
        c_in[d, s] = send(
            part(d, s), part(d, s), c_s.at[d % NZ, s], c_r.at[d % NZ, s], at(x, y, z, 1 - c)
        )

    def arrive(d):
        for s in range(SUB):
            z_in[d, s].wait_recv()
            forward(d, s)

    for s in range(SUB):
        forward(0, s)

    g_in = []
    for dy in range(1, NY):
        yy = (y + dy) % NY
        g_in.append(send(grad, gg.at[y], g_s.at[dy], g_r.at[dy], at(x, yy, z, c)))
    gg[y] = grad[...]

    def gathered(group):
        rows = []
        for d in group:
            a = t16[d % NZ, 0].reshape(64, 512)
            b = t16[d % NZ, 1].reshape(64, 512)
            rows.append(jnp.concatenate([a, b], axis=1))
        return jnp.concatenate(rows, axis=0)

    def settle(group):
        for d in group:
            for s in range(SUB):
                c_in[d, s].wait_recv()

    p_in = []

    def project(i):
        group = GROUPS[i]
        weight = jnp.concatenate(
            [
                jnp.concatenate([wg[j, 0, h * 128 : h * 128 + 128, :], wg[j, 1, h * 128 : h * 128 + 128, :]], axis=1)
                for h in range(2)
                for j in range(NX)
            ],
            axis=0,
        )
        part_p = jnp.dot(gathered(group), weight, preferred_element_type=F32).astype(B16)
        for n in range(len(group)):
            for yy in range(NY):
                r, q = n * 64 + (yy % YL) * 16, yy // YL
                ps[i, yy, n * 16 : n * 16 + 16, :] = part_p[r : r + 16, q * 128 : q * 128 + 128]
        rp[i, y] = ps[i, y]
        for dy in range(1, NY):
            yy = (y + dy) % NY
            p_in.append(
                send(ps.at[i, yy], rp.at[i, y], p_s.at[i, dy], p_r.at[i, dy], at(x, yy, z, c))
            )

    def gradient(i):
        group = GROUPS[i]
        cot = []
        for d in group:
            first = pl.multiple_of(((z + d + NZ) % NZ) * 16, 16)
            for yl in range(YL):
                cot.append(
                    jnp.concatenate(
                        [gg[yl, pl.ds(first, 16), :], gg[YL + yl, pl.ds(first, 16), :]], axis=1
                    )
                )
        cot = jnp.concatenate(cot, axis=0)
        part_w = lax.dot_general(
            gathered(group), cot, (((0,), (0,)), ((), ())), preferred_element_type=F32
        )
        for q in range(2):
            for h in range(2):
                for j in range(NX):
                    r = (h * NX + j) * 128
                    value = part_w[r : r + 128, q * 128 : q * 128 + 128]
                    if i:
                        value = value + dd[q, j, h]
                    dd[q, j, h] = value

    v_in = []
    arrive(-1)
    arrive(1)
    arrive(-2)
    arrive(2)
    for copy in w_in:
        copy.wait_recv()
    for dx in range(1, NX):
        v_in.append(
            send(wg.at[x], wg.at[x], v_s.at[dx], v_r.at[dx], at((x + dx) % NX, y, z, c))
        )
    arrive(-3)
    arrive(3)
    arrive(-4)
    arrive(4)
    for copy in v_in:
        copy.wait_recv()
    settle(GROUPS[0])
    project(0)
    arrive(-5)
    arrive(5)
    settle(GROUPS[1])
    project(1)
    arrive(-6)
    arrive(6)
    for copy in g_in:
        copy.wait_recv()
    gradient(0)
    arrive(-7)
    arrive(7)
    settle(GROUPS[2])
    gradient(1)
    project(2)
    arrive(-8)
    gradient(2)
    settle(GROUPS[3])
    gradient(3)

    d_in = []
    for k, e in enumerate((2, 6)):
        q = ((y + e) % NY) // YL
        ds[k] = dd[q].astype(B16)
        for dx in range(1, NX):
            xx = (x + dx) % NX
            d_in.append(
                send(ds.at[k, xx], rd.at[k, dx - 1], d_s.at[k, dx], d_r.at[k, dx], at(xx, y, z, c))
            )
    project(3)
    e_in = []
    for k, e in enumerate((2, 6)):
        yy = (y + e) % NY
        q = yy // YL
        total = dd[q, x]
        for dx in range(1, NX):
            d_in[k * (NX - 1) + dx - 1].wait_recv()
            total = total + rd[k, dx - 1].astype(F32)
        es[k] = total.astype(B16)
        e_in.append(
            send(es.at[k], rw.at[y // YL], e_s.at[k], e_r.at[k], at(x, yy, z, c))
        )

    for copy in p_in:
        copy.wait_recv()
    for i, group in enumerate(GROUPS):
        total = rp[i, 0].astype(F32)
        for yy in range(1, NY):
            total = total + rp[i, yy].astype(F32)
        total = total.astype(B16)
        for n, d in enumerate(group):
            first = pl.multiple_of(((z + d + NZ) % NZ) * 16, 16)
            out_p[pl.ds(first, 16), :] = total[n * 16 : n * 16 + 16, :]

    for copy in e_in:
        copy.wait_recv()
    for h in range(2):
        for b in range(2):
            r = (h * 2 + b) * 128
            out_w[r : r + 128, :] = rw[h, b]
    for copy in sent:
        copy.wait_send()


def per_device(tokens, weight_codes, block_scales, grad_out):
    vmem = pl.BlockSpec(memory_space=pltpu.VMEM)
    dma = pltpu.SemaphoreType.DMA
    return pl.pallas_call(
        kernel,
        out_shape=(
            jax.ShapeDtypeStruct((256, 128), B16),
            jax.ShapeDtypeStruct((512, 128), B16),
        ),
        in_specs=[vmem] * 4,
        out_specs=(vmem, vmem),
        scratch_shapes=[
            pltpu.VMEM((16, 16, 128), F32),
            pltpu.VMEM((16, 16, 128), B16),
            pltpu.VMEM((16, 16, 128), B16),
            pltpu.VMEM((YL, 16, 512), F32),
            pltpu.VMEM((NZ, 2, YL, 16, 512), B16),
            pltpu.VMEM((2, 256, 128), B16),
            pltpu.VMEM((NX, 2, 256, 128), B16),
            pltpu.VMEM((NY, 256, 128), B16),
            pltpu.VMEM((4, NY, 64, 128), B16),
            pltpu.VMEM((4, NY, 64, 128), B16),
            pltpu.VMEM((2, NX, 2, 128, 128), F32),
            pltpu.VMEM((2, NX, 2, 128, 128), B16),
            pltpu.VMEM((2, NX - 1, 2, 128, 128), B16),
            pltpu.VMEM((2, 2, 128, 128), B16),
            pltpu.VMEM((2, 2, 128, 128), B16),
            dma((15,)), dma((15,)),
            dma((2,)), dma((2,)),
            dma((NX,)), dma((NX,)),
            dma((NY,)), dma((NY,)),
            dma((NZ, SUB)), dma((NZ, SUB)),
            dma((NZ, SUB)), dma((NZ, SUB)),
            dma((4, NY)), dma((4, NY)),
            dma((2, NX)), dma((2, NX)),
            dma((2,)), dma((2,)),
        ],
        compiler_params=pltpu.CompilerParams(
            collective_id=0, has_side_effects=True, vmem_limit_bytes=48 << 20
        ),
    )(tokens, weight_codes, block_scales, grad_out)


def solution(mesh):
    spec = P("fsdp", "tensor")
    return jax.shard_map(
        per_device,
        mesh=mesh,
        in_specs=(P(("fsdp", "tensor"), None), spec, spec, spec),
        out_specs=(spec, spec),
        check_vma=False,
    )
```

time: 389 us -> 76.9 us (0.20)
  the two profiles are of different devices: /device:TPU:64 before, /device:TPU:1 now
where the time goes in v1:
time: 76.9 us; the launch traced here: 76.7 us
  Pallas kernels  71.4 us (93%)
  local copies, waits for them, and re-layouts  4.62 us (6%)
    pallas_call x1, Pallas kernels, per_device(): pl.pallas_call(kernel, out_shape=(jax.ShapeDtypeStruct((256, 128), B16),...  71.4 us
    unnamed x9, local copies, waits for them, and re-layouts  4.62 us

profile of v1, /device:TPU:1, one launch (start us, length us, event | category | flops | bytes accessed | tf_op | source)
XLA Modules:
  0.0 76.7 jit_solution(5215445904108645646)
XLA Ops:
  0.6 0.8 copy.6.scales
  1.4 0.0 copy-start
  1.4 0.9 %copy-done = bf16[512,128]{1,0:T(8,128)(2,1)S(1)} copy-done((bf16[512,128]{1,0:T(8,128)(2,1)S(1)}, bf16[512,128]{1,0:T(8,128)(2,1)}, u32[]{:S(2)}) %copy-start) | copy-done | bytes 131096
  2.3 0.0 copy-start.1
  2.3 0.8 %copy-done.1 = bf16[4,8192]{1,0:T(4,128)(2,1)S(1)} copy-done((bf16[4,8192]{1,0:T(4,128)(2,1)S(1)}, bf16[4,8192]{1,0:T(4,128)(2,1)}, u32[]{:S(2)}) %copy-start.1) | copy-done | bytes 65560
  3.1 0.0 copy-start.2
  3.1 0.8 %copy-done.2 = bf16[256,128]{1,0:T(8,128)(2,1)S(1)} copy-done((bf16[256,128]{1,0:T(8,128)(2,1)S(1)}, bf16[256,128]{1,0:T(8,128)(2,1)}, u32[]{:S(2)}) %copy-start.2) | copy-done | bytes 65560
  4.0 71.4 %shard_map.59 = (bf16[256,128]{1,0:T(8,128)(2,1)S(1)}, bf16[512,128]{1,0:T(8,128)(2,1)S(1)}) custom-call(bf16[4,8192]{1,0:T(4,128)(2,1)S(1)} %copy-done.1, bf16[512,128]{1,0:T(8,128)(2,1)S(1)} %copy-done, bf16[4,1]{1,0:T(4,128)(2,1)S(1)} %copy.6.scales, bf16[256,128]{1,0:T(8,128)(2,1)S(1)} %copy-done.2), custom_call_target="tpu_custom_call" | custom-call | tf_op jit(solution)/shard_map/pallas_call | solution.py:269
  75.4 0.6 copy.9
  76.0 0.7 copy.10
Async XLA Ops:
  1.4 0.9 %copy-start = (bf16[512,128]{1,0:T(8,128)(2,1)S(1)}, bf16[512,128]{1,0:T(8,128)(2,1)}, u32[]{:S(2)}) copy-start(bf16[512,128]{1,0:T(8,128)(2,1)} %codes.1) | copy-start | bytes 393220
  2.3 0.8 %copy-start.1 = (bf16[4,8192]{1,0:T(4,128)(2,1)S(1)}, bf16[4,8192]{1,0:T(4,128)(2,1)}, u32[]{:S(2)}) copy-start(bf16[4,8192]{1,0:T(4,128)(2,1)} %tok.1) | copy-start | bytes 196612
  3.1 0.8 %copy-start.2 = (bf16[256,128]{1,0:T(8,128)(2,1)S(1)}, bf16[256,128]{1,0:T(8,128)(2,1)}, u32[]{:S(2)}) copy-start(bf16[256,128]{1,0:T(8,128)(2,1)} %grad.1) | copy-start | bytes 196612

commit v2 on v1

v2 whole, which is shorter than its diff:
```python
import jax
import jax.numpy as jnp
from jax import lax
from jax.experimental import pallas as pl
from jax.experimental.pallas import tpu as pltpu
from jax.sharding import PartitionSpec as P

MESH = pl.DeviceIdType.MESH
NX, NY, NZ, YL = 4, 8, 16, 4
SUB = 2
B16, F32 = jnp.bfloat16, jnp.float32

GROUPS = ((0, -2, 2, -1, 1), (-4, 4, -3, 3), (-6, 6, -5, 5), (-8, -7, 7))
FIRST = (0, 5, 9, 13)
Z_STEPS = (1, 2)
SWAPS = [(dy, dc) for dy in range(NY) for dc in range(2) if dy or dc]


def at(x, y, z, c):
    return ((y % YL) * NX + x, z * 4 + (y // YL) * 2 + c)


def kernel(
    tok_h, codes_h, scales_h, grad_h, out_p, out_w,
    tok, codes, scales, s32, s16, a16, t32, t16, ws, wg, gg, ps, rp, dd, ds, rd, es, rw, i_s,
    a_s, a_r, w_s, w_r, v_s, v_r, g_s, g_r, z_s, z_r, c_s, c_r, p_s, p_r, d_s, d_r, e_s, e_r,
):
    f, t = lax.axis_index("fsdp"), lax.axis_index("tensor")
    x, y, z, c = f % NX, (t // 2) % 2 * YL + f // NX, t // 4, t % 2
    sent = []

    def send(src, dst, send_sem, recv_sem, device):
        copy = pltpu.make_async_remote_copy(
            src_ref=src, dst_ref=dst, send_sem=send_sem, recv_sem=recv_sem,
            device_id=device, device_id_type=MESH,
        )
        copy.start()
        sent.append(copy)
        return copy

    barrier = pltpu.get_barrier_semaphore()
    partners = [at(x, (y + dy) % NY, z, (c + dc) % 2) for dy, dc in SWAPS]
    partners += [at((x + dx) % NX, y, z, c) for dx in range(1, NX)]
    partners += [at(x, y, (z + dz) % NZ, c) for s in Z_STEPS for dz in (s, NZ - s)]
    for device in partners:
        pl.semaphore_signal(barrier, inc=1, device_id=device, device_id_type=MESH)

    loads = [
        pltpu.make_async_copy(tok_h, tok, i_s.at[0]),
        pltpu.make_async_copy(codes_h, codes, i_s.at[1]),
        pltpu.make_async_copy(scales_h, scales, i_s.at[2]),
        pltpu.make_async_copy(grad_h, gg.at[y], i_s.at[3]),
    ]
    for load in loads:
        load.start()

    loads[0].wait()
    rows = tok[...].astype(F32)
    for dest in range(2 * NY):
        yy, cc = dest // 2, dest % 2
        for j in range(NX):
            b = ((yy + 2) % YL) * 16 + j * 4 + (yy // YL) * 2 + cc
            s32[dest, j * 4 : j * 4 + 4, :] = rows[:, b * 128 : b * 128 + 128]
    s16[...] = s32[...].astype(B16)

    pl.semaphore_wait(barrier, len(partners))

    me = y * 2 + c
    swaps = []
    for k, (dy, dc) in enumerate(SWAPS):
        yy, cc = (y + dy) % NY, (c + dc) % 2
        swaps.append(
            send(s16.at[yy * 2 + cc], a16.at[me], a_s.at[k], a_r.at[k], at(x, yy, z, cc))
        )
    a16[me] = s16[me]

    loads[1].wait()
    loads[2].wait()
    scale = scales[...].astype(F32)
    for b in range(4):
        block = codes[b * 128 : b * 128 + 128, :].astype(F32) * scale[0:1, b : b + 1]
        ws[b // 2, (b % 2) * 128 : (b % 2) * 128 + 128, :] = block.astype(B16)
    loads[3].wait()

    for copy in swaps:
        copy.wait_recv()
    for src in range(2 * NY):
        yy, cc = src // 2, src % 2
        piece = a16[src].astype(F32)
        for j in range(NX):
            r = ((yy // YL) * 2 + cc) * 4
            t32[yy % YL, r : r + 4, j * 128 : j * 128 + 128] = piece[j * 4 : j * 4 + 4, :]
    t16[0, c] = t32[...].astype(B16)

    z_in, c_in = {}, {}

    def part(d, s):
        n = YL // SUB
        return t16.at[d % NZ, c, s * n : s * n + n]

    def hop(d, to, s):
        z_in[to, s] = send(
            part(d, s), part(to, s), z_s.at[to % NZ, s], z_r.at[to % NZ, s],
            at(x, y, (z + NZ + d - to) % NZ, c),
        )

    def swap(d):
        for s in range(SUB):
            c_in[d, s] = send(
                part(d, s), part(d, s), c_s.at[d % NZ, s], c_r.at[d % NZ, s], at(x, y, z, 1 - c)
            )

    def level(n):
        here = (0,) if n == 0 else ((-8,) if n == 4 else (-2 * n, 2 * n))
        ways = [(d, w) for d in here for w in ((-1, 1) if d == 0 else ((-1,) if d < 0 else (1,)))]
        for s in range(SUB):
            for d in here:
                if d:
                    z_in[d, s].wait_recv()
                for e, w in ways:
                    if e == d and abs(d + 2 * w) <= 8 and d + 2 * w != 8:
                        hop(d, d + 2 * w, s)
        for d, w in ways:
            if abs(d) < 8:
                for s in range(SUB):
                    hop(d, d + w, s)
        for d in here:
            swap(d)
        if n:
            for d in (-2 * n + 1, 2 * n - 1):
                for s in range(SUB):
                    z_in[d, s].wait_recv()
                swap(d)

    def settle(i):
        for d in GROUPS[i]:
            for s in range(SUB):
                c_in[d, s].wait_recv()

    def gathered(group):
        rows = []
        for d in group:
            a = t16[d % NZ, 0].reshape(64, 512)
            b = t16[d % NZ, 1].reshape(64, 512)
            rows.append(jnp.concatenate([a, b], axis=1))
        return jnp.concatenate(rows, axis=0)

    p_in = []

    def project(i):
        group = GROUPS[i]
        weight = jnp.concatenate(
            [
                jnp.concatenate([wg[j, 0, h * 128 : h * 128 + 128, :], wg[j, 1, h * 128 : h * 128 + 128, :]], axis=1)
                for h in range(2)
                for j in range(NX)
            ],
            axis=0,
        )
        part_p = jnp.dot(gathered(group), weight, preferred_element_type=F32).astype(B16)
        first, size = FIRST[i] * 16, len(group) * 16
        for n in range(len(group)):
            for yy in range(NY):
                r, q = n * 64 + (yy % YL) * 16, yy // YL
                ps[yy, first + n * 16 : first + n * 16 + 16, :] = part_p[r : r + 16, q * 128 : q * 128 + 128]
        rp[y, first : first + size, :] = ps[y, first : first + size, :]
        for dy in range(1, NY):
            yy = (y + dy) % NY
            p_in.append(
                send(
                    ps.at[yy, first : first + size], rp.at[y, first : first + size],
                    p_s.at[i, dy], p_r.at[i, dy], at(x, yy, z, c),
                )
            )

    def gradient(i):
        group = GROUPS[i]
        cot = []
        for d in group:
            first = pl.multiple_of(((z + d + NZ) % NZ) * 16, 16)
            for yl in range(YL):
                cot.append(
                    jnp.concatenate(
                        [gg[yl, pl.ds(first, 16), :], gg[YL + yl, pl.ds(first, 16), :]], axis=1
                    )
                )
        cot = jnp.concatenate(cot, axis=0)
        part_w = lax.dot_general(
            gathered(group), cot, (((0,), (0,)), ((), ())), preferred_element_type=F32
        )
        for q in range(2):
            for h in range(2):
                for j in range(NX):
                    r = (h * NX + j) * 128
                    value = part_w[r : r + 128, q * 128 : q * 128 + 128]
                    if i:
                        value = value + dd[q, j, h]
                    dd[q, j, h] = value

    level(0)
    w_in, v_in, g_in = [], [], {}
    for k, e in enumerate((2, 6)):
        yy = (y + e) % NY
        w_in.append(
            send(ws.at[yy // YL], wg.at[x, y // YL], w_s.at[k], w_r.at[k], at(x, yy, z, c))
        )
    level(1)

    def cotangent(d, to):
        origin = (y + NY + d) % NY
        g_in[to] = send(
            gg.at[origin], gg.at[origin], g_s.at[to % NY], g_r.at[to % NY], at(x, (y + NY + d - to) % NY, z, c)
        )

    for to in (-2, 2, -1, 1):
        cotangent(0, to)
    for copy in w_in:
        copy.wait_recv()
    for dx in (2, 1, 3):
        v_in.append(
            send(wg.at[x], wg.at[x], v_s.at[dx], v_r.at[dx], at((x + dx) % NX, y, z, c))
        )
    level(2)
    for d, to in ((-2, -4), (-2, -3), (2, 3)):
        if to != -3:
            g_in[d].wait_recv()
        cotangent(d, to)
    level(3)
    for copy in v_in:
        copy.wait_recv()
    settle(0)
    project(0)
    settle(1)
    project(1)
    for to in (-1, 1, -4, -3, 3):
        g_in[to].wait_recv()
    gradient(0)
    gradient(1)
    level(4)
    settle(2)
    gradient(2)
    settle(3)
    gradient(3)

    d_in = {}
    for k, e in enumerate((2, 6)):
        q = ((y + e) % NY) // YL
        ds[k] = dd[q].astype(B16)
        for dx in (2, 1, 3):
            xx = (x + dx) % NX
            d_in[k, dx] = send(
                ds.at[k, xx], rd.at[k, dx - 1], d_s.at[k, dx], d_r.at[k, dx], at(xx, y, z, c)
            )
    project(2)
    project(3)
    e_in = []
    for k, e in enumerate((2, 6)):
        yy = (y + e) % NY
        q = yy // YL
        total = dd[q, x]
        for dx in range(1, NX):
            d_in[k, dx].wait_recv()
            total = total + rd[k, dx - 1].astype(F32)
        es[k] = total.astype(B16)
        e_in.append(
            send(es.at[k], rw.at[y // YL], e_s.at[k], e_r.at[k], at(x, yy, z, c))
        )

    for copy in p_in:
        copy.wait_recv()
    for i, group in enumerate(GROUPS):
        for n, d in enumerate(group):
            r = (FIRST[i] + n) * 16
            total = rp[0, r : r + 16, :].astype(F32)
            for yy in range(1, NY):
                total = total + rp[yy, r : r + 16, :].astype(F32)
            first = pl.multiple_of(((z + d + NZ) % NZ) * 16, 16)
            out_p[pl.ds(first, 16), :] = total.astype(B16)

    for copy in e_in:
        copy.wait_recv()
    for h in range(2):
        for b in range(2):
            r = (h * 2 + b) * 128
            out_w[r : r + 128, :] = rw[h, b]
    for copy in sent:
        copy.wait_send()


def per_device(tokens, weight_codes, block_scales, grad_out):
    vmem = pl.BlockSpec(memory_space=pltpu.VMEM)
    dma = pltpu.SemaphoreType.DMA
    return pl.pallas_call(
        kernel,
        out_shape=(
            pltpu.VMEM((256, 128), B16),
            pltpu.VMEM((512, 128), B16),
        ),
        in_specs=[pl.BlockSpec(memory_space=pltpu.HBM)] * 4,
        out_specs=(vmem, vmem),
        scratch_shapes=[
            pltpu.VMEM((4, 8192), B16),
            pltpu.VMEM((512, 128), B16),
            pltpu.VMEM((1, 4), B16),
            pltpu.VMEM((16, 16, 128), F32),
            pltpu.VMEM((16, 16, 128), B16),
            pltpu.VMEM((16, 16, 128), B16),
            pltpu.VMEM((YL, 16, 512), F32),
            pltpu.VMEM((NZ, 2, YL, 16, 512), B16),
            pltpu.VMEM((2, 256, 128), B16),
            pltpu.VMEM((NX, 2, 256, 128), B16),
            pltpu.VMEM((NY, 256, 128), B16),
            pltpu.VMEM((NY, 256, 128), B16),
            pltpu.VMEM((NY, 256, 128), B16),
            pltpu.VMEM((2, NX, 2, 128, 128), F32),
            pltpu.VMEM((2, NX, 2, 128, 128), B16),
            pltpu.VMEM((2, NX - 1, 2, 128, 128), B16),
            pltpu.VMEM((2, 2, 128, 128), B16),
            pltpu.VMEM((2, 2, 128, 128), B16),
            dma((4,)),
            dma((15,)), dma((15,)),
            dma((2,)), dma((2,)),
            dma((NX,)), dma((NX,)),
            dma((NY,)), dma((NY,)),
            dma((NZ, SUB)), dma((NZ, SUB)),
            dma((NZ, SUB)), dma((NZ, SUB)),
            dma((4, NY)), dma((4, NY)),
            dma((2, NX)), dma((2, NX)),
            dma((2,)), dma((2,)),
        ],
        compiler_params=pltpu.CompilerParams(
            collective_id=0, has_side_effects=True, vmem_limit_bytes=60 << 20
        ),
    )(tokens, weight_codes, block_scales.T, grad_out)


def solution(mesh):
    spec = P("fsdp", "tensor")
    return jax.shard_map(
        per_device,
        mesh=mesh,
        in_specs=(P(("fsdp", "tensor"), None), spec, spec, spec),
        out_specs=(spec, spec),
        check_vma=False,
    )
```

time: 76.9 us -> 66.4 us (0.86)
  Pallas kernels: 71.4 us -> 64.3 us
  local copies, waits for them, and re-layouts: 4.62 us -> 1.29 us
    pallas_call x1, Pallas kernels: 71.4 us -> 64.3 us  [per_device(): pl.pallas_call(kernel, out_shape=(pltpu.VMEM((256, 128), B16), pltpu.VMEM...]
    unnamed x9 -> x2, local copies, waits for them, and re-layouts: 4.62 us -> 1.29 us
where the time goes in v2:
time: 66.4 us; the launch traced here: 66.2 us
  Pallas kernels  64.3 us (97%)
  local copies, waits for them, and re-layouts  1.29 us (2%)
    pallas_call x1, Pallas kernels, per_device(): pl.pallas_call(kernel, out_shape=(pltpu.VMEM((256, 128), B16), pltpu.VMEM...  64.3 us

profile of v2, /device:TPU:1, one launch (start us, length us, event | category | flops | bytes accessed | tf_op | source)
XLA Modules:
  0.0 66.2 jit_solution(7500697775803496542)
XLA Ops:
  0.6 64.3 %shard_map.59 = (bf16[256,128]{1,0:T(8,128)(2,1)S(1)}, bf16[512,128]{1,0:T(8,128)(2,1)S(1)}) custom-call(bf16[4,8192]{1,0:T(4,128)(2,1)} %tok_h.1, bf16[512,128]{1,0:T(8,128)(2,1)} %codes_h.1, bf16[1,4]{1,0:T(2,128)(2,1)} %bitcast.1, bf16[256,128]{1,0:T(8,128)(2,1)} %grad_h.1), custom_call_target="tpu_custom_call" | custom-call | tf_op jit(solution)/shard_map/pallas_call | solution.py:293
  64.9 0.6 copy.8
  65.5 0.7 copy.9

commit v3 on v2

--- a/solution.py
+++ b/solution.py
@@ -13,7 +13,8 @@
 GROUPS = ((0, -2, 2, -1, 1), (-4, 4, -3, 3), (-6, 6, -5, 5), (-8, -7, 7))
 FIRST = (0, 5, 9, 13)
 Z_STEPS = (1, 2)
-SWAPS = [(dy, dc) for dy in range(NY) for dc in range(2) if dy or dc]
+SWAPS = [(dy, dc) for dy in (4, 3, 5, 2, 6, 1, 7, 0) for dc in range(2) if dy or dc]
+PHASES = 4
 
 
 def at(x, y, z, c):
@@ -242,10 +243,13 @@
     settle(3)
     gradient(3)
 
-    d_in = {}
-    for k, e in enumerate((2, 6)):
-        q = ((y + e) % NY) // YL
-        ds[k] = dd[q].astype(B16)
+    size = 256 // PHASES
+    spans = [(k * size // 128, k * size % 128) for k in range(PHASES)]
+    d_in, e_in = {}, []
+    for k, (h, r) in enumerate(spans):
+        for j in range(NX):
+            for q in range(2):
+                ds[k, j, q] = dd[q, j, h, r : r + size, :].astype(B16)
         for dx in (2, 1, 3):
             xx = (x + dx) % NX
             d_in[k, dx] = send(
@@ -253,18 +257,22 @@
             )
     project(2)
     project(3)
-    e_in = []
-    for k, e in enumerate((2, 6)):
-        yy = (y + e) % NY
-        q = yy // YL
-        total = dd[q, x]
+    for k, (h, r) in enumerate(spans):
         for dx in range(1, NX):
             d_in[k, dx].wait_recv()
-            total = total + rd[k, dx - 1].astype(F32)
-        es[k] = total.astype(B16)
-        e_in.append(
-            send(es.at[k], rw.at[y // YL], e_s.at[k], e_r.at[k], at(x, yy, z, c))
-        )
+        for q in range(2):
+            total = dd[q, x, h, r : r + size, :]
+            for dx in range(1, NX):
+                total = total + rd[k, dx - 1, q].astype(F32)
+            es[k, q] = total.astype(B16)
+        for i, e in enumerate((2, 6)):
+            yy = (y + e) % NY
+            e_in.append(
+                send(
+                    es.at[k, yy // YL], rw.at[y // YL, h, r : r + size],
+                    e_s.at[k, i], e_r.at[k, i], at(x, yy, z, c),
+                )
+            )
 
     for copy in p_in:
         copy.wait_recv()
@@ -313,9 +321,9 @@
             pltpu.VMEM((NY, 256, 128), B16),
             pltpu.VMEM((NY, 256, 128), B16),
             pltpu.VMEM((2, NX, 2, 128, 128), F32),
-            pltpu.VMEM((2, NX, 2, 128, 128), B16),
-            pltpu.VMEM((2, NX - 1, 2, 128, 128), B16),
-            pltpu.VMEM((2, 2, 128, 128), B16),
+            pltpu.VMEM((PHASES, NX, 2, 256 // PHASES, 128), B16),
+            pltpu.VMEM((PHASES, NX - 1, 2, 256 // PHASES, 128), B16),
+            pltpu.VMEM((PHASES, 2, 256 // PHASES, 128), B16),
             pltpu.VMEM((2, 2, 128, 128), B16),
             dma((4,)),
             dma((15,)), dma((15,)),
@@ -325,8 +333,8 @@
             dma((NZ, SUB)), dma((NZ, SUB)),
             dma((NZ, SUB)), dma((NZ, SUB)),
             dma((4, NY)), dma((4, NY)),
-            dma((2, NX)), dma((2, NX)),
-            dma((2,)), dma((2,)),
+            dma((PHASES, NX)), dma((PHASES, NX)),
+            dma((PHASES, 2)), dma((PHASES, 2)),
         ],
         compiler_params=pltpu.CompilerParams(
             collective_id=0, has_side_effects=True, vmem_limit_bytes=60 << 20

time: 66.4 us -> 65.2 us (0.982)
  Pallas kernels: 64.3 us -> 63.1 us
    pallas_call x1, Pallas kernels: 64.3 us -> 63.1 us  [per_device(): pl.pallas_call(kernel, out_shape=(pltpu.VMEM((256, 128), B16), pltpu.VMEM...]
where the time goes in v3:
time: 65.2 us; the launch traced here: 65 us
  Pallas kernels  63.1 us (97%)
  local copies, waits for them, and re-layouts  1.29 us (2%)
    pallas_call x1, Pallas kernels, per_device(): pl.pallas_call(kernel, out_shape=(pltpu.VMEM((256, 128), B16), pltpu.VMEM...  63.1 us

profile of v3, /device:TPU:1, one launch (start us, length us, event | category | flops | bytes accessed | tf_op | source)
XLA Modules:
  0.0 65.0 jit_solution(3413542332740597447)
XLA Ops:
  0.6 63.1 %shard_map.59 = (bf16[256,128]{1,0:T(8,128)(2,1)S(1)}, bf16[512,128]{1,0:T(8,128)(2,1)S(1)}) custom-call(bf16[4,8192]{1,0:T(4,128)(2,1)} %tok_h.1, bf16[512,128]{1,0:T(8,128)(2,1)} %codes_h.1, bf16[1,4]{1,0:T(2,128)(2,1)} %bitcast.1, bf16[256,128]{1,0:T(8,128)(2,1)} %grad_h.1), custom_call_target="tpu_custom_call" | custom-call | tf_op jit(solution)/shard_map/pallas_call | solution.py:301
  63.7 0.6 copy.8
  64.4 0.7 %copy.9 = bf16[512,128]{1,0:T(8,128)(2,1)} copy(bf16[512,128]{1,0:T(8,128)(2,1)S(1)} %get-tuple-element.3) | data formatting | bytes 262144

commit v4 on v3

--- a/solution.py
+++ b/solution.py
@@ -237,9 +237,9 @@
         g_in[to].wait_recv()
     gradient(0)
     gradient(1)
-    level(4)
     settle(2)
     gradient(2)
+    level(4)
     settle(3)
     gradient(3)
 

time: 65.2 us -> 65.2 us (level)
  no operation moved by 1% of the time
where the time goes in v4:
time: 65.2 us; the launch traced here: 65 us
  Pallas kernels  63.1 us (97%)
  local copies, waits for them, and re-layouts  1.29 us (2%)
    pallas_call x1, Pallas kernels, per_device(): pl.pallas_call(kernel, out_shape=(pltpu.VMEM((256, 128), B16), pltpu.VMEM...  63.1 us

profile of v4, /device:TPU:1, one launch (start us, length us, event | category | flops | bytes accessed | tf_op | source)
XLA Modules:
  0.0 65.0 jit_solution(17155979134721773867)
XLA Ops:
  0.6 63.1 %shard_map.59 = (bf16[256,128]{1,0:T(8,128)(2,1)S(1)}, bf16[512,128]{1,0:T(8,128)(2,1)S(1)}) custom-call(bf16[4,8192]{1,0:T(4,128)(2,1)} %tok_h.1, bf16[512,128]{1,0:T(8,128)(2,1)} %codes_h.1, bf16[1,4]{1,0:T(2,128)(2,1)} %bitcast.1, bf16[256,128]{1,0:T(8,128)(2,1)} %grad_h.1), custom_call_target="tpu_custom_call" | custom-call | tf_op jit(solution)/shard_map/pallas_call | solution.py:301
  63.7 0.6 copy.8
  64.4 0.7 %copy.9 = bf16[512,128]{1,0:T(8,128)(2,1)} copy(bf16[512,128]{1,0:T(8,128)(2,1)S(1)} %get-tuple-element.3) | data formatting | bytes 262144
